TPU v7x, 256 devices: a whole 4x4x8 slice. The times are simulated.
256 devices in a mesh: tok: 16 (over x, z_hi, core), ch: 16 (over y, z_lo).
Axes of the slice: x: 4, y: 4, z: 8 (z_hi: 2, z_lo: 4; z = z_hi * 4 + z_lo), core: 2. Of those that a mesh axis runs over, the one named last changes fastest.
Arguments:
- tokens: bfloat16 [6144, 8192], P('tok', 'ch'), may hold values from -6 to 6
- value_weight: bfloat16 [8192, 8192], P('tok', 'ch'), may hold values from -0.0625 to 0.0625
- key_gate: bfloat16 [6144, 8192], P('tok', 'ch'), may hold values from -6 to 6
- query_gate: bfloat16 [6144, 8192], P('tok', 'ch'), may hold values from -6 to 6
- conv_filter: float32 [512, 128], P('ch'), may hold values from -0.5 to 0.5
- out_weight: bfloat16 [8192, 8192], P('tok', 'ch'), may hold values from -0.0625 to 0.0625
Outputs:
- mixed: bfloat16 [6144, 8192], P('tok', 'ch')
All inputs are finite; a program needn't handle non-finite values.
Results may differ from a plain program's by a relative error of at most 0.02.
Values may be sent and summed in bfloat16 or wider, within the bound.
A program may use at most 64 MiB of HBM per device.

v0:
```python
import jax
import jax.numpy as jnp
from jax import lax
from jax.sharding import PartitionSpec as P

TAPS = 128
GROUP = 16


def passed_along(block, axis, distance):
    devices = range(lax.axis_size(axis))
    route = [(i - distance, i) for i in devices if i - distance in devices]
    return lax.ppermute(block, axis, route)


def banded_blocks(conv_filter):
    groups_dev = conv_filter.shape[0]
    span = conv_filter.shape[1]
    period = 3 * span
    first = jnp.zeros((groups_dev, 1), jnp.float32)
    trailing = jnp.zeros((groups_dev, 2 * span - 1), jnp.float32)
    pattern = jnp.concatenate([first, conv_filter[:, ::-1], trailing], axis=1)
    tiled = jnp.tile(pattern, (1, span))
    shaped_rows = tiled[:, : span * (period - 1)].reshape(groups_dev, span, period - 1)
    return shaped_rows[:, :, : 2 * span]


def on_device(tokens, value_weight, key_gate, query_gate, conv_filter, out_weight):
    tok_rows = tokens.shape[0]
    width_dev = value_weight.shape[1]
    gathered = lax.all_gather(tokens, "ch", axis=1, tiled=True)
    columns = gathered
    values = jnp.dot(
        columns,
        lax.all_gather(value_weight, "tok", axis=0, tiled=True),
        preferred_element_type=jnp.float32,
    )
    values = values.astype(jnp.bfloat16)
    gated = (values.astype(jnp.float32) * key_gate.astype(jnp.float32)).astype(jnp.bfloat16)
    rim_rows = passed_along(gated[tok_rows - (TAPS - 1) :], "tok", 1)
    groups_dev = conv_filter.shape[0]
    leading = jnp.zeros((1, width_dev), jnp.bfloat16)
    extended = jnp.concatenate([leading, rim_rows, gated], axis=0)
    blocks_dev = tok_rows // TAPS
    stacked = extended.reshape(blocks_dev + 1, TAPS, groups_dev, GROUP)
    paired = jnp.concatenate([stacked[:-1], stacked[1:]], axis=1)
    banded = banded_blocks(conv_filter)
    banded_high = banded.astype(jnp.bfloat16)
    banded_low = (banded - banded_high.astype(jnp.float32)).astype(jnp.bfloat16)
    conv = jnp.einsum("gts,bsgc->btgc", banded_high, paired, preferred_element_type=jnp.float32)
    conv = conv + jnp.einsum(
        "gts,bsgc->btgc", banded_low, paired, preferred_element_type=jnp.float32
    )
    conv = conv.reshape(tok_rows, width_dev)
    shaped = (conv * query_gate.astype(jnp.float32)).astype(jnp.bfloat16)
    shaped_full = lax.all_gather(shaped, "ch", axis=1, tiled=True)
    columns = shaped_full
    mixed = jnp.dot(
        columns,
        lax.all_gather(out_weight, "tok", axis=0, tiled=True),
        preferred_element_type=jnp.float32,
    )
    return mixed.astype(jnp.bfloat16)


def solution(mesh):
    return jax.shard_map(
        on_device,
        mesh=mesh,
        in_specs=(
            P("tok", "ch"),
            P("tok", "ch"),
            P("tok", "ch"),
            P("tok", "ch"),
            P("ch", None),
            P("tok", "ch"),
        ),
        out_specs=P("tok", "ch"),
        check_vma=False,
    )
```

profile of v0, /device:TPU:1, one launch (start us, length us, event | category | flops | bytes accessed | tf_op | source)
XLA Modules:
  0.0 527.8 jit_solution(4946004300896583172)
XLA Ops:
  6.5 0.0 all-gather.5.cloned.1.call-start
  6.5 0.7 all-gather.5.cloned.1.call-update
  7.3 0.0 all-gather.7.cloned.1.call-start
  7.3 0.7 all-gather.7.cloned.1.call-update
  8.0 0.0 all-gather.11.cloned.1.call-start
  8.1 0.7 all-gather.11.cloned.1.call-update
  8.7 0.0 all-gather.9.cloned.1.call-start
  8.8 0.8 rev.3
  9.6 0.1 pad.2.clone
  9.7 146.9 %all-gather.5.cloned.1.call-done = bf16[384,8192]{1,0:T(8,128)(2,1)} async-done(((bf16[384,512]{1,0:T(8,128)(2,1)}), bf16[384,8192]{1,0:T(8,128)(2,1)}) %all-gather.5.cloned.1.call-update) | async-done | bytes 6291472 | tf_op jit(solution)/shard_map/all_gather | solution.py:31
  156.5 109.1 %all-gather.7.cloned.1.call-done = bf16[8192,512]{1,0:T(8,128)(2,1)} async-done(((bf16[512,512]{1,0:T(8,128)(2,1)}), bf16[8192,512]{1,0:T(8,128)(2,1)}) %all-gather.7.cloned.1.call-update) | async-done | bytes 8388624 | tf_op jit(solution)/shard_map/all_gather | solution.py:35
  265.7 8.6 %fusion.13 = bf16[384,512]{1,0:T(8,128)(2,1)S(1)} fusion(bf16[384,8192]{1,0:T(8,128)(2,1)} %all-gather.5.cloned.1.call-done, bf16[8192,512]{1,0:T(8,128)(2,1)} %all-gather.7.cloned.1.call-done, bf16[384,512]{1,0:T(8,128)(2,1)} %param.8), kind=kOutput, calls=%fused_computation.12 | convolution fusion | flops 3222208512 | bytes 15466496 | tf_op jit(solution)/shard_map/dot_general | solution.py:33
  274.3 2.1 collective-permute-start
  276.4 0.1 maximum_maximum_fusion
  276.5 0.4 tile.4
  276.9 3.6 copy.17
  280.5 3.0 slice.27
  283.5 0.0 copy-start.1
  283.5 9.7 %reshape.13 = f32[32,128,383]{2,1,0:T(8,128)} reshape(f32[32,49024]{1,0:T(8,128)} %slice.27) | data formatting | bytes 12550144 | tf_op jit(solution)/shard_map/reshape | solution.py:24
  293.2 0.0 copy-done.1
  293.2 0.2 copy.14
  293.4 0.2 copy.10
  293.7 0.1 slice.22
  293.8 0.0 collective-permute-done
  293.8 0.1 pad_maximum_fusion
  293.9 0.2 copy.9
  294.2 0.1 slice.21
  294.3 0.0 copy-start
  294.3 0.1 copy_dynamic-update-slice_fusion.1
  294.4 0.1 copy_dynamic-update-slice_fusion
  294.5 3.2 fusion.1
  297.7 0.7 copy-done
  298.4 0.8 fusion.8
  299.2 0.4 copy.13
  299.6 0.9 fusion.14
  300.5 0.0 all-gather.9.cloned.1.call-update
  300.5 72.0 %all-gather.11.cloned.1.call-done = bf16[8192,512]{1,0:T(8,128)(2,1)} async-done(((bf16[512,512]{1,0:T(8,128)(2,1)}), bf16[8192,512]{1,0:T(8,128)(2,1)}) %all-gather.11.cloned.1.call-update) | async-done | bytes 8388624 | tf_op jit(solution)/shard_map/all_gather | solution.py:60
  372.5 139.4 %all-gather.9.cloned.1.call-done = bf16[384,8192]{0,1:T(8,128)(2,1)} async-done(((bf16[384,512]{0,1:T(8,128)(2,1)}), bf16[384,8192]{0,1:T(8,128)(2,1)}) %all-gather.9.cloned.1.call-update) | async-done | bytes 6291472 | tf_op jit(solution)/shard_map/all_gather | solution.py:56
  511.9 9.4 %convolution_convert_fusion = bf16[384,512]{1,0:T(8,128)(2,1)} fusion(bf16[384,8192]{0,1:T(8,128)(2,1)} %all-gather.9.cloned.1.call-done, bf16[8192,512]{1,0:T(8,128)(2,1)} %all-gather.11.cloned.1.call-done), kind=kOutput, calls=%fused_computation.8 | convolution fusion | flops 3221422080 | bytes 15073280 | tf_op jit(solution)/shard_map/dot_general | solution.py:58
  (4 shorter events, 0.0 us)
Async XLA Ops:
  6.5 150.0 %all-gather.5.cloned.1.call-start = ((), (), s32[]{:S(2)}) async-start(), calls=%async_computation | async-start | bytes 6684672 | tf_op jit(solution)/shard_map/all_gather | solution.py:31
  7.3 258.4 %all-gather.7.cloned.1.call-start = ((), (), s32[]{:S(2)}) async-start(), calls=%async_computation.1 | async-start | bytes 8912896 | tf_op jit(solution)/shard_map/all_gather | solution.py:35
  8.0 364.5 %all-gather.11.cloned.1.call-start = ((), (), s32[]{:S(2)}) async-start(), calls=%async_computation.3 | async-start | bytes 8912896 | tf_op jit(solution)/shard_map/all_gather | solution.py:60
  8.7 503.2 %all-gather.9.cloned.1.call-start = ((), (), s32[]{:S(2)}) async-start(), calls=%async_computation.2 | async-start | bytes 6684672 | tf_op jit(solution)/shard_map/all_gather | solution.py:56
  274.3 19.5 %collective-permute-start = (bf16[127,512]{1,0:T(8,128)(2,1)S(1)}, bf16[127,512]{1,0:T(8,128)(2,1)S(1)}, u32[]{:S(2)}, u32[]{:S(2)}) collective-permute-start(bf16[127,512]{1,0:T(8,128)(2,1)S(1)} %slice.25), channel_id=1, source_target_pairs={{0,16},{16,32},{32,48},{48,64},{64,80},{80,96},{96,112},{112,128},... | collective-permute-start | bytes 390152 | tf_op jit(solution)/shard_map/ppermute | solution.py:13
  283.5 9.7 %copy-start.1 = (bf16[384,512]{1,0:T(8,128)(2,1)S(1)}, bf16[384,512]{1,0:T(8,128)(2,1)}, u32[]{:S(2)}) copy-start(bf16[384,512]{1,0:T(8,128)(2,1)} %param.9) | copy-start | bytes 1179652
  294.3 4.1 copy-start
Sparse Core Ops, SparseCore 0:
  9.1 147.3 all-gather.4
  159.2 106.4 all-gather.6
  268.3 104.1 all-gather.10
  374.1 137.7 all-gather.8
where the time goes:
time: 528 us
  waiting for transfers between devices  469 us (89%)
  matrix products  22 us (4%)
  local copies, waits for them, and re-layouts  19.8 us (4%)
  between operations  13.3 us (3%)
    all_gather x1, waiting for transfers between devices, on_device(): gathered = lax.all_gather(tokens, 'ch', axis=1, tiled=True)  147 us
    all_gather x1, waiting for transfers between devices, on_device(): shaped_full = lax.all_gather(shaped, 'ch', axis=1, tiled=True)  139 us
    all_gather x1, waiting for transfers between devices, on_device(): lax.all_gather(value_weight, 'tok', axis=0, tiled=True)  109 us
    all_gather x1, waiting for transfers between devices, on_device(): lax.all_gather(out_weight, 'tok', axis=0, tiled=True)  72 us
  transfers between devices with their start and end apart: 5, of which 4 were waited for; matrix products, arithmetic and copies ran while one was open for 6% of the time, Pallas kernels for 0%

commit v1 on v0

--- a/solution.py
+++ b/solution.py
@@ -53,7 +53,9 @@
     )
     conv = conv.reshape(tok_rows, width_dev)
     shaped = (conv * query_gate.astype(jnp.float32)).astype(jnp.bfloat16)
-    shaped_full = lax.all_gather(shaped, "ch", axis=1, tiled=True)
+    shaped_full = jnp.concatenate(
+        lax.all_to_all(jnp.stack([shaped] * lax.axis_size("ch")), "ch", 0, 0), axis=1
+    )
     columns = shaped_full
     mixed = jnp.dot(
         columns,

time: 528 us -> 510 us (0.966)
  waiting for transfers between devices: 469 us -> 443 us
  starting transfers between devices: 2.22 us -> 8.16 us
    all_gather x1 -> x0, waiting for transfers between devices: 139 us -> none  [on_device(): shaped_full = lax.all_gather(shaped, 'ch', axis=1, tiled=True)]
    all_to_all x0 -> x1, waiting for transfers between devices: none -> 99.6 us  [on_device(): lax.all_to_all(jnp.stack([shaped] * lax.axis_size('ch')), 'ch', 0, 0)]
    all_gather x1, waiting for transfers between devices: 72 us -> 85.5 us  [on_device(): lax.all_gather(out_weight, 'tok', axis=0, tiled=True)]
    all_to_all x0 -> x1, starting transfers between devices: none -> 5.98 us  [on_device(): lax.all_to_all(jnp.stack([shaped] * lax.axis_size('ch')), 'ch', 0, 0)]
  transfers between devices with their start and end apart: 5 -> 5, of which waited for: 4 -> 4; matrix products, arithmetic and copies ran while one was open for 6% -> 7% of each run, Pallas kernels for 0% -> 0%
where the time goes in v1:
time: 510 us
  waiting for transfers between devices  443 us (87%)
  local copies, waits for them, and re-layouts  23.2 us (5%)
  matrix products  22 us (4%)
  between operations  13.3 us (3%)
  starting transfers between devices  8.16 us (2%)
    all_gather x1, waiting for transfers between devices, on_device(): gathered = lax.all_gather(tokens, 'ch', axis=1, tiled=True)  147 us
    all_gather x1, waiting for transfers between devices, on_device(): lax.all_gather(value_weight, 'tok', axis=0, tiled=True)  109 us
    all_to_all x1, waiting for transfers between devices, on_device(): lax.all_to_all(jnp.stack([shaped] * lax.axis_size('ch')), 'ch', 0, 0)  99.6 us
    all_gather x1, waiting for transfers between devices, on_device(): lax.all_gather(out_weight, 'tok', axis=0, tiled=True)  85.5 us
  transfers between devices with their start and end apart: 5, of which 4 were waited for; matrix products, arithmetic and copies ran while one was open for 7% of the time, Pallas kernels for 0%

profile of v1, /device:TPU:1, one launch (start us, length us, event | category | flops | bytes accessed | tf_op | source)
XLA Modules:
  0.0 510.1 jit_solution(1525137534545216353)
XLA Ops:
  6.5 0.0 all-gather.4.cloned.1.call-start
  6.5 0.7 all-gather.4.cloned.1.call-update
  7.3 0.0 all-gather.6.cloned.1.call-start
  7.3 0.7 all-gather.6.cloned.1.call-update
  8.0 0.0 all-gather.8.cloned.1.call-start
  8.1 0.7 all-gather.8.cloned.1.call-update
  8.7 0.8 rev.3
  9.5 0.1 pad.2.clone
  9.6 146.9 %all-gather.4.cloned.1.call-done = bf16[384,8192]{1,0:T(8,128)(2,1)} async-done(((bf16[384,512]{1,0:T(8,128)(2,1)}), bf16[384,8192]{1,0:T(8,128)(2,1)}) %all-gather.4.cloned.1.call-update) | async-done | bytes 6291472 | tf_op jit(solution)/shard_map/all_gather | solution.py:31
  156.5 109.1 %all-gather.6.cloned.1.call-done = bf16[8192,512]{1,0:T(8,128)(2,1)} async-done(((bf16[512,512]{1,0:T(8,128)(2,1)}), bf16[8192,512]{1,0:T(8,128)(2,1)}) %all-gather.6.cloned.1.call-update) | async-done | bytes 8388624 | tf_op jit(solution)/shard_map/all_gather | solution.py:35
  265.7 8.6 %fusion.13 = bf16[384,512]{1,0:T(8,128)(2,1)S(1)} fusion(bf16[384,8192]{1,0:T(8,128)(2,1)} %all-gather.4.cloned.1.call-done, bf16[8192,512]{1,0:T(8,128)(2,1)} %all-gather.6.cloned.1.call-done, bf16[384,512]{1,0:T(8,128)(2,1)} %param.8), kind=kOutput, calls=%fused_computation.12 | convolution fusion | flops 3222208512 | bytes 15466496 | tf_op jit(solution)/shard_map/dot_general | solution.py:33
  274.3 2.1 collective-permute-start
  276.4 0.1 maximum_maximum_fusion
  276.5 0.4 tile.4
  276.9 3.6 copy.17
  280.5 3.0 slice.27
  283.5 0.0 copy-start.1
  283.5 9.7 %reshape.21 = f32[32,128,383]{2,1,0:T(8,128)} reshape(f32[32,49024]{1,0:T(8,128)} %slice.27) | data formatting | bytes 12550144 | tf_op jit(solution)/shard_map/reshape | solution.py:24
  293.2 0.0 copy-done.1
  293.2 0.2 copy.14
  293.5 0.2 copy.10
  293.7 0.1 slice.22
  293.8 0.0 collective-permute-done
  293.8 0.1 pad_maximum_fusion
  293.9 0.2 copy.9
  294.2 0.1 slice.21
  294.3 0.0 copy-start
  294.3 0.1 copy_dynamic-update-slice_fusion.1
  294.4 0.1 copy_dynamic-update-slice_fusion
  294.5 3.2 fusion.1
  297.7 0.7 copy-done
  298.4 0.8 fusion.8
  299.2 0.4 copy.13
  299.7 0.1 fusion.14
  299.8 3.4 stack.2
  303.2 6.0 %all-to-all-start = ((bf16[16,384,512]{1,2,0:T(8,128)(2,1)}), bf16[16,384,512]{1,2,0:T(8,128)(2,1)}, u32[]{:S(2)}, u32[]{:S(2)}) async-start(bf16[16,384,512]{1,2,0:T(8,128)(2,1)} %stack.2), calls=%async_computation | async-start | bytes 12582912 | tf_op jit(solution)/shard_map/all_to_all | solution.py:57
  309.2 85.5 %all-gather.8.cloned.1.call-done = bf16[8192,512]{1,0:T(8,128)(2,1)} async-done(((bf16[512,512]{1,0:T(8,128)(2,1)}), bf16[8192,512]{1,0:T(8,128)(2,1)}) %all-gather.8.cloned.1.call-update) | async-done | bytes 8388624 | tf_op jit(solution)/shard_map/all_gather | solution.py:62
  394.6 99.6 %all-to-all-done = bf16[16,384,512]{1,2,0:T(8,128)(2,1)} async-done(((bf16[16,384,512]{1,2,0:T(8,128)(2,1)}), bf16[16,384,512]{1,2,0:T(8,128)(2,1)}, u32[]{:S(2)}, u32[]{:S(2)}) %all-to-all-start) | async-done | bytes 6291488 | tf_op jit(solution)/shard_map/all_to_all | solution.py:57
  494.2 9.4 %convolution_convert_fusion = bf16[384,512]{1,0:T(8,128)(2,1)} fusion(bf16[384,8192]{0,1:T(8,128)(2,1)} %bitcast.6, bf16[8192,512]{1,0:T(8,128)(2,1)} %all-gather.8.cloned.1.call-done), kind=kOutput, calls=%fused_computation.8 | convolution fusion | flops 3221422080 | bytes 15073280 | tf_op jit(solution)/shard_map/dot_general | solution.py:60
  (4 shorter events, 0.0 us)
Async XLA Ops:
  6.5 150.0 %all-gather.4.cloned.1.call-start = ((), (), s32[]{:S(2)}) async-start(), calls=%async_computation.1 | async-start | bytes 6684672 | tf_op jit(solution)/shard_map/all_gather | solution.py:31
  7.3 258.4 %all-gather.6.cloned.1.call-start = ((), (), s32[]{:S(2)}) async-start(), calls=%async_computation.2 | async-start | bytes 8912896 | tf_op jit(solution)/shard_map/all_gather | solution.py:35
  8.0 386.6 %all-gather.8.cloned.1.call-start = ((), (), s32[]{:S(2)}) async-start(), calls=%async_computation.3 | async-start | bytes 8912896 | tf_op jit(solution)/shard_map/all_gather | solution.py:62
  274.3 19.5 %collective-permute-start = (bf16[127,512]{1,0:T(8,128)(2,1)S(1)}, bf16[127,512]{1,0:T(8,128)(2,1)S(1)}, u32[]{:S(2)}, u32[]{:S(2)}) collective-permute-start(bf16[127,512]{1,0:T(8,128)(2,1)S(1)} %slice.25), channel_id=1, source_target_pairs={{0,16},{16,32},{32,48},{48,64},{64,80},{80,96},{96,112},{112,128},... | collective-permute-start | bytes 390152 | tf_op jit(solution)/shard_map/ppermute | solution.py:13
  283.5 9.7 %copy-start.1 = (bf16[384,512]{1,0:T(8,128)(2,1)S(1)}, bf16[384,512]{1,0:T(8,128)(2,1)}, u32[]{:S(2)}) copy-start(bf16[384,512]{1,0:T(8,128)(2,1)} %param.9) | copy-start | bytes 1179652
  294.3 4.1 copy-start
  303.2 191.1 %all-to-all-start = ((bf16[16,384,512]{1,2,0:T(8,128)(2,1)}), bf16[16,384,512]{1,2,0:T(8,128)(2,1)}, u32[]{:S(2)}, u32[]{:S(2)}) async-start(bf16[16,384,512]{1,2,0:T(8,128)(2,1)} %stack.2), calls=%async_computation | async-start | bytes 12582912 | tf_op jit(solution)/shard_map/all_to_all | solution.py:57
Sparse Core Ops, SparseCore 0:
  9.1 147.3 all-gather.3
  159.2 106.4 all-gather.5
  268.3 126.2 all-gather.7
